TPU v7x, 1024 devices: a whole 4x4x32 slice. The times are simulated.
1024 devices in a mesh: runs: 64 (over z_lo, x), feat: 16 (over y, z_hi, core).
Axes of the slice: x: 4, y: 4, z: 32 (z_hi: 2, z_lo: 16; z = z_hi * 16 + z_lo), core: 2. Of those that a mesh axis runs over, the one named last changes fastest.
Arguments:
- samples: bfloat16 [2560, 24576], P('runs', 'feat'), may hold values from -12 to 12, as said below
Outputs:
- markov: float32 [2560, 2560], P('runs', 'feat')
Inputs may be any that keep to these rules, and one draw needn't show every extreme that they name: `samples`: real-valued deformation features.
All inputs are finite; a program needn't handle non-finite values.
Results may differ from a plain program's by a relative error of at most 0.0003.
Values may be sent and summed in bfloat16 or wider, within the bound.
A program may use at most 32 MiB of HBM per device.

v0:
```python
import jax
import jax.numpy as jnp
from jax import lax
from jax.sharding import PartitionSpec as P

FEATURES = 24576


def spread_stat(values):
    rows = values.shape[0]
    total = rows * lax.axis_size("runs")
    placed = jnp.zeros((total,), jnp.float32)
    placed = lax.dynamic_update_slice_in_dim(placed, values, lax.axis_index("runs") * rows, 0)
    return lax.psum(placed, ("runs", "feat"))


def per_device(samples):
    rows = samples.shape[0]
    total = rows * lax.axis_size("runs")
    width = total // lax.axis_size("feat")
    wide = samples.astype(jnp.float32)
    local_sq = jnp.sum(wide * wide, axis=1)
    partial_value = lax.dot_general(
        samples,
        lax.all_gather(samples, "runs", axis=0, tiled=True),
        (((1,), (1,)), ((), ())),
        preferred_element_type=jnp.float32,
    )
    gram = lax.psum_scatter(partial_value, "feat", scatter_dimension=1, tiled=True)
    row_start = lax.axis_index("runs") * rows
    col_start = lax.axis_index("feat") * width
    norms = spread_stat(local_sq)
    row_norm = lax.dynamic_slice_in_dim(norms, row_start, rows, 0)
    col_norm = lax.dynamic_slice_in_dim(norms, col_start, width, 0)
    dist = row_norm[:, None] + col_norm[None, :] - 2.0 * gram
    kernel = jnp.exp(-dist / (4.0 * FEATURES))
    density = spread_stat(jnp.sum(kernel, axis=1))
    row_density = lax.dynamic_slice_in_dim(density, row_start, rows, 0)
    col_density = lax.dynamic_slice_in_dim(density, col_start, width, 0)
    scaled = kernel / (row_density[:, None] * col_density[None, :])
    degree = lax.psum(jnp.sum(scaled, axis=1), "feat")
    return total * 1.0 * scaled / degree[:, None]


def solution(mesh):
    placed = (P("runs", "feat"),)
    return jax.shard_map(
        per_device, mesh=mesh, in_specs=placed, out_specs=P("runs", "feat"), check_vma=False
    )
```

profile of v0, /device:TPU:1, one launch (start us, length us, event | category | flops | bytes accessed | tf_op | source)
XLA Modules:
  0.0 1191.6 jit_solution(6593294612487476112)
XLA Ops:
  6.5 0.0 copy-start
  6.5 0.0 all-gather.2.cloned.1.call-start
  6.5 0.7 all-gather.2.cloned.1.call-update
  7.3 0.0 reduce-scatter.4.cloned.1.call-start
  7.3 686.3 %all-gather.2.cloned.1.call-done = bf16[2560,1536]{1,0:T(8,128)(2,1)} async-done(((bf16[40,1536]{1,0:T(8,128)(2,1)}), bf16[2560,1536]{1,0:T(8,128)(2,1)}) %all-gather.2.cloned.1.call-update) | async-done | bytes 7864336 | tf_op jit(solution)/shard_map/all_gather | solution.py:25
  693.6 6.7 convolution_bitcast_fusion
  700.2 0.0 reduce-scatter.4.cloned.1.call-update
  700.3 0.0 copy-done
  700.3 0.1 multiply_reduce_fusion
  700.4 0.3 dynamic_update_slice.6
  700.7 225.6 %psum.21 = f32[2560]{0:T(1024)S(1)} all-reduce(f32[2560]{0:T(1024)S(1)} %dynamic_update_slice.6), channel_id=1, replica_groups=mesh['runs'=64,'feat'=16] {'runs','feat'}, use_global_device_ids=true, to_apply=%region_1.0 | all-reduce | flops 2560 | bytes 20480 | tf_op jit(solution)/shard_map/psum | solution.py:14
  926.3 0.1 dynamic_slice.12
  926.4 0.1 dynamic_slice.13
  926.5 0.0 reduce-scatter.4.cloned.1.call-done
  926.5 0.9 copy.3
  927.4 0.2 fusion
  927.6 0.3 dynamic_update_slice.7
  927.9 155.3 %psum.22 = f32[2560]{0:T(1024)S(1)} all-reduce(f32[2560]{0:T(1024)S(1)} %dynamic_update_slice.7), channel_id=1, replica_groups=mesh['runs'=64,'feat'=16] {'runs','feat'}, use_global_device_ids=true, to_apply=%region_4.0 | all-reduce | flops 2560 | bytes 20480 | tf_op jit(solution)/shard_map/psum | solution.py:14
  1083.2 0.1 dynamic_slice.14
  1083.3 0.1 dynamic_slice.15
  1083.3 0.2 fusion.1
  1083.5 100.5 %psum.23 = f32[40]{0:T(128)S(1)} all-reduce(f32[40]{0:T(128)S(1)} %get-tuple-element.5), channel_id=1, replica_groups=mesh['runs'=64,'feat'=16] {'feat'}, use_global_device_ids=true, to_apply=%region_6.0 | all-reduce | flops 40 | bytes 320 | tf_op jit(solution)/shard_map/psum | solution.py:41
  1184.0 0.7 multiply_divide_fusion
  (2 shorter events, 0.0 us)
Async XLA Ops:
  6.5 693.7 %copy-start = (bf16[40,1536]{1,0:T(8,128)(2,1)S(1)}, bf16[40,1536]{1,0:T(8,128)(2,1)}, u32[]{:S(2)}) copy-start(bf16[40,1536]{1,0:T(8,128)(2,1)} %param.1) | copy-start | bytes 368644
  6.5 687.0 %all-gather.2.cloned.1.call-start = ((), (), s32[]{:S(2)}) async-start(), calls=%async_computation.1 | async-start | bytes 7987200 | tf_op jit(solution)/shard_map/all_gather | solution.py:25
  7.3 919.2 %reduce-scatter.4.cloned.1.call-start = ((), (), s32[]{:S(2)}) async-start(), calls=%async_computation.2 | async-start | bytes 1392640
Sparse Core Ops, SparseCore 0:
  10.0 683.5 all-gather.1
  700.4 211.8 reduce-scatter.3
where the time goes:
time: 1210 us; the launch traced here: 1190 us
  waiting for transfers between devices  687 us (57%)
  blocking collectives  481 us (40%)
  between operations  13.4 us (1%)
    all_gather x1, waiting for transfers between devices, per_device(): lax.all_gather(samples, 'runs', axis=0, tiled=True)  686 us
    psum x2, blocking collectives, spread_stat(): return lax.psum(placed, ('runs', 'feat'))  381 us
    psum x1, blocking collectives, per_device(): degree = lax.psum(jnp.sum(scaled, axis=1), 'feat')  101 us
  transfers between devices with their start and end apart: 2, of which 1 were waited for; matrix products, arithmetic and copies ran while one was open for 0% of the time, Pallas kernels for 0%

commit v1 on v0

v1 whole, which is shorter than its diff:
```python
import functools

import jax
import jax.numpy as jnp
from jax import lax
from jax.experimental import pallas as pl
from jax.experimental.pallas import tpu as pltpu
from jax.sharding import PartitionSpec as P

MESH = pl.DeviceIdType.MESH
F32 = jnp.float32
NT = (((1,), (1,)), ((), ()))


def device(x, z, y, h, c):
    return (z * 4 + x, (y * 2 + h) * 2 + c)


def kernel(
    total, scale, s_ref, o_ref, abuf, bbuf, acat, bcat, tbuf, r1buf, swsend, owsend, swbuf, owbuf, d1buf, d2buf, gbuf,
    a_ss, a_rs, x_ss, x_rs, b_ss, b_rs, r1_ss, r1_rs, sw_ss, sw_rs, ow_ss, ow_rs, d1_ss, d1_rs, d2_ss, d2_rs, g_ss, g_rs,
):
    run, feat = lax.axis_index("runs"), lax.axis_index("feat")
    x, z = run % 4, run // 4
    u, v = z // 4, z % 4
    y, h, c = feat // 4, (feat // 2) % 2, feat % 2

    def copy(src, dst, ss, rs, to):
        return pltpu.make_async_remote_copy(
            src_ref=src, dst_ref=dst, send_sem=ss, recv_sem=rs, device_id=to, device_id_type=MESH
        )

    def is_me(to):
        return jnp.logical_and(to[0] == run, to[1] == feat)

    here = (run, feat)
    fv = 2 * h + c
    swap_c = jnp.where(u <= y, 0, 1)
    own_c = jnp.where(y < u, 0, 1)
    swap_from = [device(x, y * 4 + v, fv, hh, swap_c) for hh in range(2)]
    own_from = [[device(xx, u * 4 + fv, v, hh, own_c) for xx in range(4)] for hh in range(2)]
    swap_ok = [jnp.where(c == 0, u2 <= u, u2 > u) for u2 in range(4)]
    own_ok = [jnp.where(c == 0, u2 < u, u2 >= u) for u2 in range(4)]
    tile_ok = [jnp.where(c == 0, u2 <= u, u2 >= u) for u2 in range(4)]
    swap_to = [device(x, u2 * 4 + v, u, y // 2, y % 2) for u2 in range(4)]
    own_to = [[device(xx, u * 4 + y, u2, v // 2, v % 2) for xx in range(4)] for u2 in range(4)]

    near = [((x + dx) % 4, (v + dv) % 4) for dv in range(4) for dx in range(4) if (dx, dv) != (0, 0)]
    near_dev = [device(xx, u * 4 + vv, y, h, c) for xx, vv in near]
    us = [(u + d) % 4 for d in range(1, 4)]
    u_dev = [device(x, uu * 4 + v, y, h, c) for uu in us]
    fs = [(feat + d) % 16 for d in range(1, 16)]

    barrier = pltpu.get_barrier_semaphore()
    for to in near_dev + u_dev + [(run, ff) for ff in fs]:
        pl.semaphore_signal(barrier, inc=1, device_id=to, device_id_type=MESH)
    mine = 0
    for to in swap_from + own_from[0] + own_from[1]:
        same = is_me(to)
        mine = mine + jnp.where(same, 1, 0)

        @pl.when(jnp.logical_not(same))
        def _():
            pl.semaphore_signal(barrier, inc=1, device_id=to, device_id_type=MESH)

    pl.semaphore_wait(barrier, 33 + jnp.where(c == 0, 5 * u + 1, 19 - 5 * u) - mine)

    def b_out(i):
        return copy(s_ref, bbuf.at[u], b_ss.at[i], b_rs.at[u], u_dev[i])

    def b_sends(i):
        return jnp.where(c == 0, us[i] > u, us[i] < u)

    def a_out(d):
        return copy(s_ref, abuf.at[v, x], a_ss.at[d], a_rs.at[v], device(x, u * 4 + (v + d) % 4, y, h, c))

    def x_out(d, e):
        vv = (v + d) % 4
        src = s_ref if d == 0 else abuf.at[vv, x]
        return copy(src, abuf.at[vv, x], x_ss.at[d, e], x_rs.at[vv, x], device((x + e) % 4, z, y, h, c))

    for d in (1, 3, 2):
        a_out(d).start()
    for i in range(3):
        pl.when(b_sends(i))(b_out(i).start)
    for e in (1, 3, 2):
        x_out(0, e).start()
    abuf[v, x] = s_ref[...]
    bbuf[u] = s_ref[...]
    for d in (1, 3, 2):
        vv = (v + d) % 4
        copy(s_ref, abuf.at[vv, x], a_ss.at[d], a_rs.at[vv], here).wait_recv()
        for e in (1, 3, 2):
            x_out(d, e).start()
    for d in (0, 1, 3, 2):
        vv = (v + d) % 4
        for e in range(1, 4):
            xx = (x + e) % 4
            copy(s_ref, abuf.at[vv, xx], x_ss.at[d, e], x_rs.at[vv, xx], here).wait_recv()

    ones = jnp.ones((8, s_ref.shape[1]), jnp.bfloat16)
    norms = []
    for vv in range(4):
        wide = jnp.concatenate([abuf[vv, xx].astype(F32) for xx in range(4)], axis=0)
        acat[vv] = wide.astype(jnp.bfloat16)
        square = wide * wide
        high = square.astype(jnp.bfloat16)
        low = (square - high.astype(F32)).astype(jnp.bfloat16)
        norm = lax.dot_general(ones, high, NT, preferred_element_type=F32)
        norm = norm + lax.dot_general(ones, low, NT, preferred_element_type=F32)
        norms.append(norm[0:1])

    for i in range(3):
        uu = us[i]

        @pl.when(jnp.where(c == 0, uu < u, uu > u))
        def _():
            copy(s_ref, bbuf.at[uu], b_ss.at[i], b_rs.at[uu], here).wait_recv()

        @pl.when(jnp.where(c == 0, uu > u, uu < u))
        def _():
            bbuf[uu] = s_ref[...]

    wide = jnp.concatenate([bbuf[uu].astype(F32) for uu in range(4)], axis=0)
    bcat[...] = wide.astype(jnp.bfloat16)
    rownorm = jnp.sum(wide * wide, axis=1, keepdims=True)

    def r1_out(vv, u2):
        return copy(tbuf.at[vv, u2], r1buf.at[y, u2], r1_ss.at[vv, u2], r1_rs.at[y, u2], device(x, z, vv, h, c))

    for vv in range(4):
        gram = lax.dot_general(bcat[...], acat[vv], NT, preferred_element_type=F32)
        part = rownorm + norms[vv] - 2.0 * gram
        for u2 in range(4):
            tbuf[vv, u2] = part[u2 * 40 : u2 * 40 + 40]

        @pl.when(vv != y)
        def _():
            for u2 in range(4):
                pl.when(tile_ok[u2])(r1_out(vv, u2).start)

    for d in range(1, 4):
        yy = (y + d) % 4
        for u2 in range(4):

            @pl.when(tile_ok[u2])
            def _():
                copy(tbuf.at[0, u2], r1buf.at[yy, u2], r1_ss.at[0, u2], r1_rs.at[yy, u2], here).wait_recv()

    def sw_out(u2):
        return copy(swsend.at[u2], swbuf.at[h], sw_ss.at[u2], sw_rs.at[h], swap_to[u2])

    def ow_out(u2, xx):
        return copy(owsend.at[u2, xx], owbuf.at[h, x], ow_ss.at[u2, xx], ow_rs.at[h, x], own_to[u2][xx])

    for u2 in range(4):

        @pl.when(tile_ok[u2])
        def _():
            tile = tbuf[y, u2]
            for d in range(1, 4):
                tile = tile + r1buf[(y + d) % 4, u2]
            swsend[u2] = tile
            turned = tile.T
            for xx in range(4):
                owsend[u2, xx] = turned[xx * 40 : xx * 40 + 40]

        same = is_me(swap_to[u2])

        @pl.when(jnp.logical_and(swap_ok[u2], same))
        def _():
            swbuf[h] = swsend[u2]

        pl.when(jnp.logical_and(swap_ok[u2], jnp.logical_not(same)))(sw_out(u2).start)
        for xx in range(4):
            same = is_me(own_to[u2][xx])

            @pl.when(jnp.logical_and(own_ok[u2], same))
            def _():
                owbuf[h, x] = owsend[u2, xx]

            pl.when(jnp.logical_and(own_ok[u2], jnp.logical_not(same)))(ow_out(u2, xx).start)

    for hh in range(2):

        @pl.when(jnp.logical_not(is_me(swap_from[hh])))
        def _():
            copy(swsend.at[0], swbuf.at[hh], sw_ss.at[0], sw_rs.at[hh], here).wait_recv()

        for xx in range(4):

            @pl.when(jnp.logical_not(is_me(own_from[hh][xx])))
            def _():
                copy(owsend.at[0, 0], owbuf.at[hh, xx], ow_ss.at[0, 0], ow_rs.at[hh, xx], here).wait_recv()

    own = jnp.concatenate([owbuf[0, xx] + owbuf[1, xx] for xx in range(4)], axis=1)
    dist = swbuf[0] + swbuf[1] + own
    value = jnp.exp(-dist / scale)

    def d1_out(i):
        return copy(d1buf.at[v, x], d1buf.at[v, x], d1_ss.at[i], d1_rs.at[v, x], near_dev[i])

    d1buf[v, x] = jnp.sum(value, axis=0, keepdims=True)
    for i in range(15):
        d1_out(i).start()
    for xx, vv in near:
        copy(d1buf.at[v, x], d1buf.at[vv, xx], d1_ss.at[0], d1_rs.at[vv, xx], here).wait_recv()
    density = d1buf[0, 0]
    for i in range(1, 16):
        density = density + d1buf[i // 4, i % 4]

    def d2_out(i):
        return copy(d2buf.at[u], d2buf.at[u], d2_ss.at[i], d2_rs.at[u], u_dev[i])

    d2buf[u] = density
    for i in range(3):
        d2_out(i).start()
    for uu in us:
        copy(d2buf.at[u], d2buf.at[uu], d2_ss.at[0], d2_rs.at[uu], here).wait_recv()
    density = d2buf[0] + d2buf[1] + d2buf[2] + d2buf[3]

    scaled = value / density
    degree = jnp.sum(scaled, axis=1, keepdims=True)

    def g_out(i):
        return copy(gbuf.at[feat], gbuf.at[feat], g_ss.at[i], g_rs.at[feat], (run, fs[i]))

    gbuf[feat] = jnp.broadcast_to(degree, (40, 128)).T[0:1]
    for i in range(15):
        g_out(i).start()
    for ff in fs:
        copy(gbuf.at[feat], gbuf.at[ff], g_ss.at[0], g_rs.at[ff], here).wait_recv()
    degree = gbuf[0]
    for i in range(1, 16):
        degree = degree + gbuf[i]
    degree = jnp.broadcast_to(degree, (128, 40)).T[:, 0:1]
    o_ref[...] = total * scaled / degree

    for d in range(1, 4):
        a_out(d).wait_send()
    for i in range(3):
        pl.when(b_sends(i))(b_out(i).wait_send)
        d2_out(i).wait_send()
    for d in range(4):
        for e in range(1, 4):
            x_out(d, e).wait_send()
    for vv in range(4):

        @pl.when(vv != y)
        def _():
            for u2 in range(4):
                pl.when(tile_ok[u2])(r1_out(vv, u2).wait_send)

    for u2 in range(4):
        ok = jnp.logical_and(swap_ok[u2], jnp.logical_not(is_me(swap_to[u2])))
        pl.when(ok)(sw_out(u2).wait_send)
        for xx in range(4):
            ok = jnp.logical_and(own_ok[u2], jnp.logical_not(is_me(own_to[u2][xx])))
            pl.when(ok)(ow_out(u2, xx).wait_send)
    for i in range(15):
        d1_out(i).wait_send()
        g_out(i).wait_send()


def per_device(samples):
    rows, width = samples.shape
    total = 1.0 * rows * lax.axis_size("runs")
    scale = 4.0 * width * lax.axis_size("feat")
    dma = pltpu.SemaphoreType.DMA
    vm = pltpu.VMEM
    bf = jnp.bfloat16
    return pl.pallas_call(
        functools.partial(kernel, total, scale),
        out_shape=jax.ShapeDtypeStruct((rows, 4 * rows), F32),
        in_specs=[pl.BlockSpec(memory_space=pltpu.VMEM)],
        out_specs=pl.BlockSpec(memory_space=pltpu.VMEM),
        scratch_shapes=[
            vm((4, 4, rows, width), bf),
            vm((4, rows, width), bf),
            vm((4, 4 * rows, width), bf),
            vm((4 * rows, width), bf),
            vm((4, 4, rows, 4 * rows), F32),
            vm((4, 4, rows, 4 * rows), F32),
            vm((4, rows, 4 * rows), F32),
            vm((4, 4, rows, rows), F32),
            vm((2, rows, 4 * rows), F32),
            vm((2, 4, rows, rows), F32),
            vm((4, 4, 1, 4 * rows), F32),
            vm((4, 1, 4 * rows), F32),
            vm((16, 1, rows), F32),
            dma((4,)), dma((4,)),
            dma((4, 4)), dma((4, 4)),
            dma((3,)), dma((4,)),
            dma((4, 4)), dma((4, 4)),
            dma((4,)), dma((2,)),
            dma((4, 4)), dma((2, 4)),
            dma((15,)), dma((4, 4)),
            dma((3,)), dma((4,)),
            dma((15,)), dma((16,)),
        ],
        compiler_params=pltpu.CompilerParams(
            collective_id=0, has_side_effects=True, vmem_limit_bytes=48 << 20
        ),
        name="markov",
    )(samples)


def solution(mesh):
    placed = P("runs", "feat")
    return jax.shard_map(per_device, mesh=mesh, in_specs=(placed,), out_specs=placed, check_vma=False)
```

time: 1210 us -> 149 us (0.12); the launches traced: 1190 us -> 149 us
  waiting for transfers between devices: 687 us -> 0 us
  blocking collectives: 481 us -> 0 us
  Pallas kernels: 0 us -> 147 us
  between operations: 13.4 us -> 0.01 us
    all_gather x1 -> x0, waiting for transfers between devices: 686 us -> none  [per_device(): lax.all_gather(samples, 'runs', axis=0, tiled=True)]
    psum x3 -> x0, blocking collectives: 481 us -> none  [the longest x2 381 us: spread_stat(): return lax.psum(placed, ('runs', 'feat'))]
    pallas_call x0 -> x1, Pallas kernels: none -> 147 us  [per_device(): pl.pallas_call(functools.partial(kernel, total, scale), out_shape=jax.Sha...]
  transfers between devices with their start and end apart: 2 -> 0, of which waited for: 1 -> 0; matrix products, arithmetic and copies ran while one was open for 0% -> 0% of each run, Pallas kernels for 0% -> 0%
where the time goes in v1:
time: 149 us
  Pallas kernels  147 us (99%)
  local copies, waits for them, and re-layouts  1.52 us (1%)
    pallas_call x1, Pallas kernels, per_device(): pl.pallas_call(functools.partial(kernel, total, scale), out_shape=jax.Sha...  147 us

profile of v1, /device:TPU:1, one launch (start us, length us, event | category | flops | bytes accessed | tf_op | source)
XLA Modules:
  0.0 148.6 jit_solution(15733835808602110676)
XLA Ops:
  0.0 0.0 copy-start
  0.0 0.9 copy-done
  0.9 147.1 %markov.1 = f32[40,160]{1,0:T(8,128)S(1)} custom-call(bf16[40,1536]{1,0:T(8,128)(2,1)S(1)} %copy-done), custom_call_target="tpu_custom_call" | custom-call | tf_op jit(solution)/shard_map/markov/pallas_call | solution.py:272
  148.0 0.6 copy.3
Async XLA Ops:
  0.0 0.9 copy-start

commit v2 on v1

--- a/solution.py
+++ b/solution.py
@@ -17,8 +17,8 @@
 
 
 def kernel(
-    total, scale, s_ref, o_ref, abuf, bbuf, acat, bcat, tbuf, r1buf, swsend, owsend, swbuf, owbuf, d1buf, d2buf, gbuf,
-    a_ss, a_rs, x_ss, x_rs, b_ss, b_rs, r1_ss, r1_rs, sw_ss, sw_rs, ow_ss, ow_rs, d1_ss, d1_rs, d2_ss, d2_rs, g_ss, g_rs,
+    total, scale, s_ref, o_ref, abuf, bbuf, acat, bcat, tbuf, r1buf, hsend, hbuf, swsend, owsend, swbuf, owbuf, d1buf, d2buf, gbuf,
+    a_ss, a_rs, x_ss, x_rs, b_ss, b_rs, r1_ss, r1_rs, h_ss, h_rs, sw_ss, sw_rs, ow_ss, ow_rs, d1_ss, d1_rs, d2_ss, d2_rs, g_ss, g_rs,
 ):
     run, feat = lax.axis_index("runs"), lax.axis_index("feat")
     x, z = run % 4, run // 4
@@ -34,25 +34,34 @@
         return jnp.logical_and(to[0] == run, to[1] == feat)
 
     here = (run, feat)
-    fv = 2 * h + c
+    def nearest(other):
+        return jnp.where(jnp.abs(other - u) == 3, 1 - h, h)
+
     swap_c = jnp.where(u <= y, 0, 1)
     own_c = jnp.where(y < u, 0, 1)
-    swap_from = [device(x, y * 4 + v, fv, hh, swap_c) for hh in range(2)]
-    own_from = [[device(xx, u * 4 + fv, v, hh, own_c) for xx in range(4)] for hh in range(2)]
+    swap_from = [device(x, y * 4 + v, 2 * b + c, nearest(y), swap_c) for b in range(2)]
+    own_from = [[device(xx, u * 4 + 2 * b + c, v, h, own_c) for xx in range(4)] for b in range(2)]
     swap_ok = [jnp.where(c == 0, u2 <= u, u2 > u) for u2 in range(4)]
     own_ok = [jnp.where(c == 0, u2 < u, u2 >= u) for u2 in range(4)]
     tile_ok = [jnp.where(c == 0, u2 <= u, u2 >= u) for u2 in range(4)]
-    swap_to = [device(x, u2 * 4 + v, u, y // 2, y % 2) for u2 in range(4)]
-    own_to = [[device(xx, u * 4 + y, u2, v // 2, v % 2) for xx in range(4)] for u2 in range(4)]
+    swap_to = [device(x, u2 * 4 + v, u, nearest(u2), y % 2) for u2 in range(4)]
+    own_to = [[device(xx, u * 4 + y, u2, h, v % 2) for xx in range(4)] for u2 in range(4)]
 
     near = [((x + dx) % 4, (v + dv) % 4) for dv in range(4) for dx in range(4) if (dx, dv) != (0, 0)]
     near_dev = [device(xx, u * 4 + vv, y, h, c) for xx, vv in near]
     us = [(u + d) % 4 for d in range(1, 4)]
     u_dev = [device(x, uu * 4 + v, y, h, c) for uu in us]
-    fs = [(feat + d) % 16 for d in range(1, 16)]
+    other = device(x, z, y, 1 - h, c)
+    plane = [((y + d // 2) % 4, (c + d) % 2) for d in range(1, 8)]
+    plane_dev = [device(x, z, yy, h, cc) for yy, cc in plane]
+    w = 4 * h + u
+    ring_to = [(w + d) % 8 for d in (1, 7, 2)]
+    ring_from = [(w + d) % 8 for d in (7, 1, 6)]
+    ring_to_dev = [device(x, ww % 4 * 4 + v, y, ww // 4, c) for ww in ring_to]
+    ring_from_dev = [device(x, ww % 4 * 4 + v, y, ww // 4, c) for ww in ring_from]
 
     barrier = pltpu.get_barrier_semaphore()
-    for to in near_dev + u_dev + [(run, ff) for ff in fs]:
+    for to in near_dev + u_dev + [other] + plane_dev + ring_from_dev:
         pl.semaphore_signal(barrier, inc=1, device_id=to, device_id_type=MESH)
     mine = 0
     for to in swap_from + own_from[0] + own_from[1]:
@@ -63,7 +72,7 @@
         def _():
             pl.semaphore_signal(barrier, inc=1, device_id=to, device_id_type=MESH)
 
-    pl.semaphore_wait(barrier, 33 + jnp.where(c == 0, 5 * u + 1, 19 - 5 * u) - mine)
+    pl.semaphore_wait(barrier, 29 + jnp.where(c == 0, 5 * u + 1, 19 - 5 * u) - mine)
 
     def b_out(i):
         return copy(s_ref, bbuf.at[u], b_ss.at[i], b_rs.at[u], u_dev[i])
@@ -125,41 +134,52 @@
     bcat[...] = wide.astype(jnp.bfloat16)
     rownorm = jnp.sum(wide * wide, axis=1, keepdims=True)
 
-    def r1_out(vv, u2):
-        return copy(tbuf.at[vv, u2], r1buf.at[y, u2], r1_ss.at[vv, u2], r1_rs.at[y, u2], device(x, z, vv, h, c))
-
+    def r1_out(vv, k):
+        return copy(tbuf.at[vv, k], r1buf.at[y, k], r1_ss.at[vv, k], r1_rs.at[y, k], device(x, z, vv, h, c))
+
+    slot_ok = tile_ok + [u >= 0]
     for vv in range(4):
         gram = lax.dot_general(bcat[...], acat[vv], NT, preferred_element_type=F32)
         part = rownorm + norms[vv] - 2.0 * gram
         for u2 in range(4):
-            tbuf[vv, u2] = part[u2 * 40 : u2 * 40 + 40]
+            tbuf[vv, u2] = part[u2 * 40 : u2 * 40 + 40, :128]
+        tbuf[vv, 4] = jnp.concatenate([part[u2 * 40 : u2 * 40 + 40, 128:] for u2 in range(4)], axis=1)
 
         @pl.when(vv != y)
         def _():
-            for u2 in range(4):
-                pl.when(tile_ok[u2])(r1_out(vv, u2).start)
-
-    for d in range(1, 4):
-        yy = (y + d) % 4
-        for u2 in range(4):
-
-            @pl.when(tile_ok[u2])
-            def _():
-                copy(tbuf.at[0, u2], r1buf.at[yy, u2], r1_ss.at[0, u2], r1_rs.at[yy, u2], here).wait_recv()
+            for k in range(5):
+                pl.when(slot_ok[k])(r1_out(vv, k).start)
+
+    def h_out(k):
+        return copy(hsend.at[k], hbuf.at[k], h_ss.at[k], h_rs.at[k], other)
+
+    for k in range(5):
+
+        @pl.when(slot_ok[k])
+        def _():
+            for d in range(1, 4):
+                yy = (y + d) % 4
+                copy(tbuf.at[0, k], r1buf.at[yy, k], r1_ss.at[0, k], r1_rs.at[yy, k], here).wait_recv()
+            tile = tbuf[y, k]
+            for d in range(1, 4):
+                tile = tile + r1buf[(y + d) % 4, k]
+            hsend[k] = tile
+            h_out(k).start()
 
     def sw_out(u2):
-        return copy(swsend.at[u2], swbuf.at[h], sw_ss.at[u2], sw_rs.at[h], swap_to[u2])
+        return copy(swsend.at[u2], swbuf.at[y // 2], sw_ss.at[u2], sw_rs.at[y // 2], swap_to[u2])
 
     def ow_out(u2, xx):
-        return copy(owsend.at[u2, xx], owbuf.at[h, x], ow_ss.at[u2, xx], ow_rs.at[h, x], own_to[u2][xx])
-
+        return copy(owsend.at[u2, xx], owbuf.at[v // 2, x], ow_ss.at[u2, xx], ow_rs.at[v // 2, x], own_to[u2][xx])
+
+    copy(hsend.at[4], hbuf.at[4], h_ss.at[4], h_rs.at[4], other).wait_recv()
+    rest = hsend[4] + hbuf[4]
     for u2 in range(4):
 
         @pl.when(tile_ok[u2])
         def _():
-            tile = tbuf[y, u2]
-            for d in range(1, 4):
-                tile = tile + r1buf[(y + d) % 4, u2]
+            copy(hsend.at[u2], hbuf.at[u2], h_ss.at[u2], h_rs.at[u2], other).wait_recv()
+            tile = jnp.concatenate([hsend[u2] + hbuf[u2], rest[:, u2 * 32 : u2 * 32 + 32]], axis=1)
             swsend[u2] = tile
             turned = tile.T
             for xx in range(4):
@@ -169,7 +189,7 @@
 
         @pl.when(jnp.logical_and(swap_ok[u2], same))
         def _():
-            swbuf[h] = swsend[u2]
+            swbuf[y // 2] = swsend[u2]
 
         pl.when(jnp.logical_and(swap_ok[u2], jnp.logical_not(same)))(sw_out(u2).start)
         for xx in range(4):
@@ -177,30 +197,32 @@
 
             @pl.when(jnp.logical_and(own_ok[u2], same))
             def _():
-                owbuf[h, x] = owsend[u2, xx]
+                owbuf[v // 2, x] = owsend[u2, xx]
 
             pl.when(jnp.logical_and(own_ok[u2], jnp.logical_not(same)))(ow_out(u2, xx).start)
 
-    for hh in range(2):
-
-        @pl.when(jnp.logical_not(is_me(swap_from[hh])))
-        def _():
-            copy(swsend.at[0], swbuf.at[hh], sw_ss.at[0], sw_rs.at[hh], here).wait_recv()
+    for b in range(2):
+
+        @pl.when(jnp.logical_not(is_me(swap_from[b])))
+        def _():
+            copy(swsend.at[0], swbuf.at[b], sw_ss.at[0], sw_rs.at[b], here).wait_recv()
 
         for xx in range(4):
 
-            @pl.when(jnp.logical_not(is_me(own_from[hh][xx])))
+            @pl.when(jnp.logical_not(is_me(own_from[b][xx])))
             def _():
-                copy(owsend.at[0, 0], owbuf.at[hh, xx], ow_ss.at[0, 0], ow_rs.at[hh, xx], here).wait_recv()
-
-    own = jnp.concatenate([owbuf[0, xx] + owbuf[1, xx] for xx in range(4)], axis=1)
-    dist = swbuf[0] + swbuf[1] + own
-    value = jnp.exp(-dist / scale)
+                copy(owsend.at[0, 0], owbuf.at[b, xx], ow_ss.at[0, 0], ow_rs.at[b, xx], here).wait_recv()
+
+    values = []
+    for b in range(2):
+        own = jnp.concatenate([owbuf[b, xx] for xx in range(4)], axis=1)
+        values.append(jnp.exp(-(swbuf[b] + own) / scale))
 
     def d1_out(i):
         return copy(d1buf.at[v, x], d1buf.at[v, x], d1_ss.at[i], d1_rs.at[v, x], near_dev[i])
 
-    d1buf[v, x] = jnp.sum(value, axis=0, keepdims=True)
+    for b in range(2):
+        d1buf[v, x, b] = jnp.sum(values[b], axis=0, keepdims=True)
     for i in range(15):
         d1_out(i).start()
     for xx, vv in near:
@@ -210,7 +232,7 @@
         density = density + d1buf[i // 4, i % 4]
 
     def d2_out(i):
-        return copy(d2buf.at[u], d2buf.at[u], d2_ss.at[i], d2_rs.at[u], u_dev[i])
+        return copy(d2buf.at[u], d2buf.at[u], d2_ss.at[i], d2_rs.at[u], ring_to_dev[i])
 
     d2buf[u] = density
     for i in range(3):
@@ -219,22 +241,23 @@
         copy(d2buf.at[u], d2buf.at[uu], d2_ss.at[0], d2_rs.at[uu], here).wait_recv()
     density = d2buf[0] + d2buf[1] + d2buf[2] + d2buf[3]
 
-    scaled = value / density
-    degree = jnp.sum(scaled, axis=1, keepdims=True)
+    scaled = [values[b] / density[b] for b in range(2)]
+    degree = jnp.sum(scaled[0], axis=1, keepdims=True) + jnp.sum(scaled[1], axis=1, keepdims=True)
+    place = 2 * y + c
 
     def g_out(i):
-        return copy(gbuf.at[feat], gbuf.at[feat], g_ss.at[i], g_rs.at[feat], (run, fs[i]))
-
-    gbuf[feat] = jnp.broadcast_to(degree, (40, 128)).T[0:1]
-    for i in range(15):
+        return copy(gbuf.at[place], gbuf.at[place], g_ss.at[i], g_rs.at[place], plane_dev[i])
+
+    gbuf[place] = jnp.broadcast_to(degree, (40, 128)).T[0:1]
+    for i in range(7):
         g_out(i).start()
-    for ff in fs:
-        copy(gbuf.at[feat], gbuf.at[ff], g_ss.at[0], g_rs.at[ff], here).wait_recv()
+    for yy, cc in plane:
+        copy(gbuf.at[place], gbuf.at[2 * yy + cc], g_ss.at[0], g_rs.at[2 * yy + cc], here).wait_recv()
     degree = gbuf[0]
-    for i in range(1, 16):
+    for i in range(1, 8):
         degree = degree + gbuf[i]
     degree = jnp.broadcast_to(degree, (128, 40)).T[:, 0:1]
-    o_ref[...] = total * scaled / degree
+    o_ref[...] = total * jnp.where(h == 0, scaled[0], scaled[1]) / degree
 
     for d in range(1, 4):
         a_out(d).wait_send()
@@ -248,8 +271,8 @@
 
         @pl.when(vv != y)
         def _():
-            for u2 in range(4):
-                pl.when(tile_ok[u2])(r1_out(vv, u2).wait_send)
+            for k in range(5):
+                pl.when(slot_ok[k])(r1_out(vv, k).wait_send)
 
     for u2 in range(4):
         ok = jnp.logical_and(swap_ok[u2], jnp.logical_not(is_me(swap_to[u2])))
@@ -257,8 +280,11 @@
         for xx in range(4):
             ok = jnp.logical_and(own_ok[u2], jnp.logical_not(is_me(own_to[u2][xx])))
             pl.when(ok)(ow_out(u2, xx).wait_send)
+    for k in range(5):
+        pl.when(slot_ok[k])(h_out(k).wait_send)
     for i in range(15):
         d1_out(i).wait_send()
+    for i in range(7):
         g_out(i).wait_send()
 
 
@@ -279,24 +305,27 @@
             vm((4, rows, width), bf),
             vm((4, 4 * rows, width), bf),
             vm((4 * rows, width), bf),
-            vm((4, 4, rows, 4 * rows), F32),
-            vm((4, 4, rows, 4 * rows), F32),
+            vm((4, 5, rows, 128), F32),
+            vm((4, 5, rows, 128), F32),
+            vm((5, rows, 128), F32),
+            vm((5, rows, 128), F32),
             vm((4, rows, 4 * rows), F32),
             vm((4, 4, rows, rows), F32),
             vm((2, rows, 4 * rows), F32),
             vm((2, 4, rows, rows), F32),
-            vm((4, 4, 1, 4 * rows), F32),
-            vm((4, 1, 4 * rows), F32),
-            vm((16, 1, rows), F32),
+            vm((4, 4, 2, 1, 4 * rows), F32),
+            vm((4, 2, 1, 4 * rows), F32),
+            vm((8, 1, rows), F32),
             dma((4,)), dma((4,)),
             dma((4, 4)), dma((4, 4)),
             dma((3,)), dma((4,)),
-            dma((4, 4)), dma((4, 4)),
+            dma((4, 5)), dma((4, 5)),
+            dma((5,)), dma((5,)),
             dma((4,)), dma((2,)),
             dma((4, 4)), dma((2, 4)),
             dma((15,)), dma((4, 4)),
             dma((3,)), dma((4,)),
-            dma((15,)), dma((16,)),
+            dma((7,)), dma((8,)),
         ],
         compiler_params=pltpu.CompilerParams(
             collective_id=0, has_side_effects=True, vmem_limit_bytes=48 << 20

time: 149 us -> 121 us (0.81)
  Pallas kernels: 147 us -> 119 us
    pallas_call x1, Pallas kernels: 147 us -> 119 us  [per_device(): pl.pallas_call(functools.partial(kernel, total, scale), out_shape=jax.Sha...]
where the time goes in v2:
time: 121 us
  Pallas kernels  119 us (98%)
  local copies, waits for them, and re-layouts  1.52 us (1%)
    pallas_call x1, Pallas kernels, per_device(): pl.pallas_call(functools.partial(kernel, total, scale), out_shape=jax.Sha...  119 us

profile of v2, /device:TPU:1, one launch (start us, length us, event | category | flops | bytes accessed | tf_op | source)
XLA Modules:
  0.0 120.9 jit_solution(4028200080667984503)
XLA Ops:
  0.0 0.0 copy-start
  0.0 0.9 copy-done
  0.9 119.4 %markov.1 = f32[40,160]{1,0:T(8,128)S(1)} custom-call(bf16[40,1536]{1,0:T(8,128)(2,1)S(1)} %copy-done), custom_call_target="tpu_custom_call" | custom-call | tf_op jit(solution)/shard_map/markov/pallas_call | solution.py:298
  120.3 0.6 copy.3
Async XLA Ops:
  0.0 0.9 copy-start

commit v3 on v2

v3 whole, which is shorter than its diff:
```python
import functools

import jax
import jax.numpy as jnp
from jax import lax
from jax.experimental import pallas as pl
from jax.experimental.pallas import tpu as pltpu
from jax.sharding import PartitionSpec as P

MESH = pl.DeviceIdType.MESH
F32 = jnp.float32
BF16 = jnp.bfloat16
NT = (((1,), (1,)), ((), ()))


def device(x, z, y, h, c):
    return (z * 4 + x, (y * 2 + h) * 2 + c)


def pack(tile):
    rest = tile[:, 128:]
    first = jnp.concatenate([rest[i * 8 : i * 8 + 8] for i in range(4)], axis=1)
    second = jnp.concatenate([rest[32:40], jnp.zeros((8, 96), F32)], axis=1)
    return jnp.concatenate([tile[:, :128], first, second], axis=0)


def unpack(packed):
    rest = [packed[40:48, i * 32 : i * 32 + 32] for i in range(4)] + [packed[48:56, :32]]
    return jnp.concatenate([packed[:40], jnp.concatenate(rest, axis=0)], axis=1)


def kernel(
    total, scale, s_ref, o_ref, abuf, bbuf, acat, anorm, tbuf, r1buf, hsend, hbuf, swsend, owsend, swbuf, owbuf,
    d1buf, d2buf, gbuf, a_ss, a_rs, x_ss, x_rs, b_ss, b_rs, r1_ss, r1_rs, h_ss, h_rs, sw_ss, sw_rs, ow_ss, ow_rs,
    d1_ss, d1_rs, d2_ss, d2_rs, g_ss, g_rs, up_sem, down_sem, plane_sem,
):
    run, feat = lax.axis_index("runs"), lax.axis_index("feat")
    x, z = run % 4, run // 4
    u, v = z // 4, z % 4
    y, h, c = feat // 4, (feat // 2) % 2, feat % 2
    here = (run, feat)

    def copy(src, dst, ss, rs, to):
        return pltpu.make_async_remote_copy(
            src_ref=src, dst_ref=dst, send_sem=ss, recv_sem=rs, device_id=to, device_id_type=MESH
        )

    def signal(sem, to):
        pl.semaphore_signal(sem, inc=1, device_id=to, device_id_type=MESH)

    def is_me(to):
        return jnp.logical_and(to[0] == run, to[1] == feat)

    both = jnp.logical_and
    no = jnp.logical_not

    steps = jnp.where(c == 0, u + 1, 4 - u)
    way = jnp.where(c == 0, 1, -1)
    passes = jnp.where(c == 0, u < 3, u > 0)

    def u2(k):
        return u - way * k

    def nearest(other):
        return jnp.where(jnp.abs(other - u) == 3, 1 - h, h)

    swap_c = jnp.where(u <= y, 0, 1)
    own_c = jnp.where(y < u, 0, 1)
    swap_from = [device(x, y * 4 + v, 2 * b + c, nearest(y), swap_c) for b in range(2)]
    own_from = [[device(xx, u * 4 + 2 * b + c, v, h, own_c) for xx in range(4)] for b in range(2)]

    def swap_to(k):
        return device(x, u2(k) * 4 + v, u, nearest(u2(k)), y % 2)

    def own_to(k, xx):
        return device(xx, u * 4 + y, u2(k), h, v % 2)

    near = [((x + dx) % 4, (v + dv) % 4) for dv in range(4) for dx in range(4) if (dx, dv) != (0, 0)]
    near_dev = [device(xx, u * 4 + vv, y, h, c) for xx, vv in near]
    us = [(u + d) % 4 for d in range(1, 4)]
    other = device(x, z, y, 1 - h, c)
    plane = [((y + d // 2) % 4, (c + d) % 2) for d in range(1, 8)]
    plane_dev = [device(x, z, yy, h, cc) for yy, cc in plane]
    w = 4 * h + u
    ring = [(w + d) % 8 for d in (1, 7, 2)]
    above, below, above2 = [device(x, ww % 4 * 4 + v, y, ww // 4, c) for ww in ring]
    ring_to = [above, below, above2]

    barrier = pltpu.get_barrier_semaphore()
    for to in near_dev + [above, below] + plane_dev:
        signal(barrier, to)
    mine = 0
    for to in own_from[0] + own_from[1]:
        same = is_me(to)
        mine = mine + jnp.where(same, 1, 0)

        @pl.when(no(same))
        def _():
            signal(barrier, to)

    pl.semaphore_wait(barrier, 24 + 4 * jnp.where(c == 0, u, 4 - u) - mine)

    def b_out(k):
        src = s_ref if isinstance(k, int) and k == 0 else bbuf.at[u2(k)]
        to = device(x, (u + way) * 4 + v, y, h, c)
        return copy(src, bbuf.at[u2(k)], b_ss.at[k], b_rs.at[u2(k)], to)

    def b_in(k):
        return copy(s_ref, bbuf.at[u2(k)], b_ss.at[0], b_rs.at[u2(k)], here)

    def a_out(d):
        return copy(s_ref, abuf.at[v, x], a_ss.at[d], a_rs.at[v], device(x, u * 4 + (v + d) % 4, y, h, c))

    def x_out(d, e):
        vv = (v + d) % 4
        src = s_ref if d == 0 else abuf.at[vv, x]
        return copy(src, abuf.at[vv, x], x_ss.at[d, e], x_rs.at[vv, x], device((x + e) % 4, z, y, h, c))

    def relay_b(k):
        @pl.when(k < steps)
        def _():
            b_in(k).wait_recv()
            pl.when(passes)(b_out(k).start)

    def relay_a(d):
        vv = (v + d) % 4
        copy(s_ref, abuf.at[vv, x], a_ss.at[d], a_rs.at[vv], here).wait_recv()
        for e in (1, 3, 2):
            x_out(d, e).start()

    def take_a(d):
        vv = (v + d) % 4
        for e in range(1, 4):
            xx = (x + e) % 4
            copy(s_ref, abuf.at[vv, xx], x_ss.at[d, e], x_rs.at[vv, xx], here).wait_recv()
        wide = jnp.concatenate([abuf[vv, xx].astype(F32) for xx in range(4)], axis=0)
        acat[vv] = wide.astype(BF16)
        norm = jnp.sum(wide * wide, axis=1, keepdims=True)
        anorm[vv] = jnp.broadcast_to(norm, (norm.shape[0], 128)).T[0:1]

    pl.when(passes)(b_out(0).start)
    for d in (1, 3, 2):
        a_out(d).start()
    for e in (1, 3, 2):
        x_out(0, e).start()
    signal(up_sem, above)
    signal(down_sem.at[0], below)
    abuf[v, x] = s_ref[...]
    bbuf[u] = s_ref[...]
    relay_a(1)
    relay_a(3)
    pl.semaphore_wait(up_sem, 1)
    pl.semaphore_wait(down_sem.at[0], 1)
    signal(down_sem.at[1], below)
    for to in plane_dev:
        signal(plane_sem, to)
    relay_b(1)
    relay_a(2)
    take_a(0)
    pl.semaphore_wait(down_sem.at[1], 1)
    signal(down_sem.at[2], below)
    relay_b(2)
    take_a(1)
    take_a(3)
    take_a(2)

    pl.semaphore_wait(down_sem.at[2], 1)
    pl.semaphore_wait(plane_sem, 7)

    def r1_out(vv, k):
        return copy(tbuf.at[vv, k], r1buf.at[y, k], r1_ss.at[vv, k], r1_rs.at[y, k], device(x, z, vv, h, c))

    def h_out(k):
        return copy(hsend.at[k], hbuf.at[k], h_ss.at[k], h_rs.at[k], other)

    def reduce_y(k):
        for d in range(1, 4):
            yy = (y + d) % 4
            copy(tbuf.at[0, k], r1buf.at[yy, k], r1_ss.at[0, k], r1_rs.at[yy, k], here).wait_recv()
        tile = tbuf[y, k]
        for d in range(1, 4):
            tile = tile + r1buf[(y + d) % 4, k]
        hsend[k] = tile
        h_out(k).start()

    def tiles(k, carry):
        pl.when(k == 3)(lambda: b_in(k).wait_recv())
        block = bbuf[u2(k)]
        wide = block.astype(F32)
        norm = jnp.sum(wide * wide, axis=1, keepdims=True)
        for vv in range(4):
            gram = lax.dot_general(block, acat[vv], NT, preferred_element_type=F32)
            tbuf[vv, k] = pack(norm + anorm[vv] - 2.0 * gram)
            pl.when(vv != y)(r1_out(vv, k).start)
        pl.when(k > 0)(lambda: reduce_y(k - 1))
        return carry

    lax.fori_loop(0, steps, tiles, 0)
    reduce_y(steps - 1)

    def sw_out(k):
        return copy(swsend.at[k], swbuf.at[y // 2], sw_ss.at[k], sw_rs.at[y // 2], swap_to(k))

    def ow_out(k, xx):
        return copy(owsend.at[k, xx], owbuf.at[v // 2, x], ow_ss.at[k, xx], ow_rs.at[v // 2, x], own_to(k, xx))

    def swaps(k):
        return jnp.logical_or(c == 0, k > 0)

    def owns(k):
        return jnp.logical_or(c == 1, k > 0)

    def place(k, carry):
        copy(hsend.at[k], hbuf.at[k], h_ss.at[k], h_rs.at[k], other).wait_recv()
        packed = hsend[k] + hbuf[k]
        swsend[k] = packed
        same = is_me(swap_to(k))

        @pl.when(both(swaps(k), same))
        def _():
            swbuf[y // 2] = swsend[k]

        pl.when(both(swaps(k), no(same)))(sw_out(k).start)

        @pl.when(owns(k))
        def _():
            turned = unpack(packed).T
            for xx in range(4):
                owsend[k, xx] = turned[xx * 40 : xx * 40 + 40]
                same = is_me(own_to(k, xx))

                @pl.when(same)
                def _():
                    owbuf[v // 2, x] = owsend[k, xx]

                pl.when(no(same))(ow_out(k, xx).start)

        return carry

    lax.fori_loop(0, steps, place, 0)

    for b in range(2):

        @pl.when(no(is_me(swap_from[b])))
        def _():
            copy(swsend.at[0], swbuf.at[b], sw_ss.at[0], sw_rs.at[b], here).wait_recv()

        for xx in range(4):

            @pl.when(no(is_me(own_from[b][xx])))
            def _():
                copy(owsend.at[0, 0], owbuf.at[b, xx], ow_ss.at[0, 0], ow_rs.at[b, xx], here).wait_recv()

    values = []
    for b in range(2):
        own = jnp.concatenate([owbuf[b, xx] for xx in range(4)], axis=1)
        values.append(jnp.exp(-(unpack(swbuf[b]) + own) / scale))

    def d1_out(i):
        return copy(d1buf.at[v, x], d1buf.at[v, x], d1_ss.at[i], d1_rs.at[v, x], near_dev[i])

    for b in range(2):
        d1buf[v, x, b] = jnp.sum(values[b], axis=0, keepdims=True)
    for i in range(15):
        d1_out(i).start()
    for xx, vv in near:
        copy(d1buf.at[v, x], d1buf.at[vv, xx], d1_ss.at[0], d1_rs.at[vv, xx], here).wait_recv()
    density = d1buf[0, 0]
    for i in range(1, 16):
        density = density + d1buf[i // 4, i % 4]

    def d2_out(i):
        return copy(d2buf.at[u], d2buf.at[u], d2_ss.at[i], d2_rs.at[u], ring_to[i])

    d2buf[u] = density
    for i in range(3):
        d2_out(i).start()
    for uu in us:
        copy(d2buf.at[u], d2buf.at[uu], d2_ss.at[0], d2_rs.at[uu], here).wait_recv()
    density = d2buf[0] + d2buf[1] + d2buf[2] + d2buf[3]

    scaled = [values[b] / density[b] for b in range(2)]
    degree = jnp.sum(scaled[0], axis=1, keepdims=True) + jnp.sum(scaled[1], axis=1, keepdims=True)
    place = 2 * y + c

    def g_out(i):
        return copy(gbuf.at[place], gbuf.at[place], g_ss.at[i], g_rs.at[place], plane_dev[i])

    gbuf[place] = jnp.broadcast_to(degree, (40, 128)).T[0:1]
    for i in range(7):
        g_out(i).start()
    for yy, cc in plane:
        copy(gbuf.at[place], gbuf.at[2 * yy + cc], g_ss.at[0], g_rs.at[2 * yy + cc], here).wait_recv()
    degree = gbuf[0]
    for i in range(1, 8):
        degree = degree + gbuf[i]
    degree = jnp.broadcast_to(degree, (128, 40)).T[:, 0:1]
    o_ref[...] = total * jnp.where(h == 0, scaled[0], scaled[1]) / degree

    for d in range(1, 4):
        a_out(d).wait_send()
    for d in range(4):
        for e in range(1, 4):
            x_out(d, e).wait_send()
    for k in range(3):
        pl.when(both(passes, k < steps))(b_out(k).wait_send)

    def sent_tiles(k, carry):
        for vv in range(4):
            pl.when(vv != y)(r1_out(vv, k).wait_send)
        h_out(k).wait_send()
        return carry

    lax.fori_loop(0, steps, sent_tiles, 0)

    def sent_places(k, carry):
        pl.when(both(swaps(k), no(is_me(swap_to(k)))))(sw_out(k).wait_send)
        for xx in range(4):
            pl.when(both(owns(k), no(is_me(own_to(k, xx)))))(ow_out(k, xx).wait_send)
        return carry

    lax.fori_loop(0, steps, sent_places, 0)

    for i in range(15):
        d1_out(i).wait_send()
    for i in range(3):
        d2_out(i).wait_send()

    for i in range(7):
        g_out(i).wait_send()


def per_device(samples):
    rows, width = samples.shape
    total = 1.0 * rows * lax.axis_size("runs")
    scale = 4.0 * width * lax.axis_size("feat")
    dma = pltpu.SemaphoreType.DMA
    regular = pltpu.SemaphoreType.REGULAR
    vm = pltpu.VMEM
    return pl.pallas_call(
        functools.partial(kernel, total, scale),
        out_shape=jax.ShapeDtypeStruct((rows, 4 * rows), F32),
        in_specs=[pl.BlockSpec(memory_space=pltpu.VMEM)],
        out_specs=pl.BlockSpec(memory_space=pltpu.VMEM),
        scratch_shapes=[
            vm((4, 4, rows, width), BF16),
            vm((4, rows, width), BF16),
            vm((4, 4 * rows, width), BF16),
            vm((4, 1, 4 * rows), F32),
            vm((4, 4, 56, 128), F32),
            vm((4, 4, 56, 128), F32),
            vm((4, 56, 128), F32),
            vm((4, 56, 128), F32),
            vm((4, 56, 128), F32),
            vm((4, 4, rows, rows), F32),
            vm((2, 56, 128), F32),
            vm((2, 4, rows, rows), F32),
            vm((4, 4, 2, 1, 4 * rows), F32),
            vm((4, 2, 1, 4 * rows), F32),
            vm((8, 1, rows), F32),
            dma((4,)), dma((4,)),
            dma((4, 4)), dma((4, 4)),
            dma((3,)), dma((4,)),
            dma((4, 4)), dma((4, 4)),
            dma((4,)), dma((4,)),
            dma((4,)), dma((2,)),
            dma((4, 4)), dma((2, 4)),
            dma((15,)), dma((4, 4)),
            dma((3,)), dma((4,)),
            dma((7,)), dma((8,)),
            regular, regular((3,)), regular,
        ],
        compiler_params=pltpu.CompilerParams(
            collective_id=0, has_side_effects=True, vmem_limit_bytes=48 << 20
        ),
        name="markov",
    )(samples)


def solution(mesh):
    placed = P("runs", "feat")
    return jax.shard_map(per_device, mesh=mesh, in_specs=(placed,), out_specs=placed, check_vma=False)
```

time: 121 us -> 108 us (0.89)
  Pallas kernels: 119 us -> 106 us
    pallas_call x1, Pallas kernels: 119 us -> 106 us  [per_device(): pl.pallas_call(functools.partial(kernel, total, scale), out_shape=jax.Sha...]
where the time goes in v3:
time: 108 us
  Pallas kernels  106 us (98%)
  local copies, waits for them, and re-layouts  1.52 us (1%)
    pallas_call x1, Pallas kernels, per_device(): pl.pallas_call(functools.partial(kernel, total, scale), out_shape=jax.Sha...  106 us

profile of v3, /device:TPU:1, one launch (start us, length us, event | category | flops | bytes accessed | tf_op | source)
XLA Modules:
  0.0 107.5 jit_solution(10480130886505898216)
XLA Ops:
  0.0 0.0 copy-start
  0.0 0.9 copy-done
  0.9 106.0 %markov.1 = f32[40,160]{1,0:T(8,128)S(1)} custom-call(bf16[40,1536]{1,0:T(8,128)(2,1)S(1)} %copy-done), custom_call_target="tpu_custom_call" | custom-call | tf_op jit(solution)/shard_map/markov/pallas_call | solution.py:340
  106.9 0.6 copy.3
Async XLA Ops:
  0.0 0.9 copy-start

commit v4 on v3

v4 whole, which is shorter than its diff:
```python
import functools

import jax
import jax.numpy as jnp
from jax import lax
from jax.experimental import pallas as pl
from jax.experimental.pallas import tpu as pltpu
from jax.sharding import PartitionSpec as P

MESH = pl.DeviceIdType.MESH
F32 = jnp.float32
BF16 = jnp.bfloat16
NT = (((1,), (1,)), ((), ()))


def device(x, z, y, h, c):
    return (z * 4 + x, (y * 2 + h) * 2 + c)


def pack(tile):
    last = jnp.concatenate([tile[112:], jnp.zeros((8, 40), F32)], axis=0)
    return jnp.concatenate([tile[:56], tile[56:112], last, jnp.zeros((56, 8), F32)], axis=1)


def unpack(packed):
    return jnp.concatenate([packed[:, :40], packed[:, 40:80], packed[:48, 80:120]], axis=0)


def pack_quarter(part):
    first = jnp.concatenate([part[:8], part[8:16], part[16:24], jnp.zeros((8, 8), F32)], axis=1)
    second = jnp.concatenate([part[24:32], part[32:], jnp.zeros((8, 48), F32)], axis=1)
    return jnp.concatenate([first, second], axis=0)


def unpack_quarter(packed):
    pieces = [packed[:8, i * 40 : i * 40 + 40] for i in range(3)] + [packed[8:, i * 40 : i * 40 + 40] for i in range(2)]
    return jnp.concatenate(pieces, axis=0)


def kernel(
    total, scale, s_ref, o_ref, abuf, bbuf, acat, anorm, bnorm, tbuf, r1buf, hsend, hbuf, swsend, owsend, swbuf, owbuf,
    d1buf, d2buf, gbuf, a_ss, a_rs, x_ss, x_rs, b_ss, b_rs, r1_ss, r1_rs, h_ss, h_rs, sw_ss, sw_rs, ow_ss, ow_rs,
    d1_ss, d1_rs, d2_ss, d2_rs, g_ss, g_rs, up_sem, down_sem, plane_sem, side_sem,
    near_sem, in_sem,
):
    run, feat = lax.axis_index("runs"), lax.axis_index("feat")
    x, z = run % 4, run // 4
    u, v = z // 4, z % 4
    y, h, c = feat // 4, (feat // 2) % 2, feat % 2
    here = (run, feat)

    def copy(src, dst, ss, rs, to):
        return pltpu.make_async_remote_copy(
            src_ref=src, dst_ref=dst, send_sem=ss, recv_sem=rs, device_id=to, device_id_type=MESH
        )

    def signal(sem, to):
        pl.semaphore_signal(sem, inc=1, device_id=to, device_id_type=MESH)

    def is_me(to):
        return jnp.logical_and(to[0] == run, to[1] == feat)

    both = jnp.logical_and
    no = jnp.logical_not

    steps = jnp.where(c == 0, u + 1, 4 - u)
    way = jnp.where(c == 0, 1, -1)
    passes = jnp.where(c == 0, u < 3, u > 0)

    def u2(k):
        return u - way * k

    def nearest(other):
        return jnp.where(jnp.abs(other - u) == 3, 1 - h, h)

    swap_c = jnp.where(u <= y, 0, 1)
    own_c = jnp.where(y < u, 0, 1)
    swap_from = [device(x, y * 4 + v, 2 * b + c, nearest(y), swap_c) for b in range(2)]
    own_from = [[device(xx, u * 4 + 2 * b + c, v, h, own_c) for xx in range(4)] for b in range(2)]

    def swap_to(k):
        return device(x, u2(k) * 4 + v, u, nearest(u2(k)), y % 2)

    def own_to(k, xx):
        return device(xx, u * 4 + y, u2(k), h, v % 2)

    near = [((x + dx) % 4, (v + dv) % 4) for dv in range(4) for dx in range(4) if (dx, dv) != (0, 0)]
    near_dev = [device(xx, u * 4 + vv, y, h, c) for xx, vv in near]
    other = device(x, z, y, 1 - h, c)
    plane = [((y + d // 2) % 4, (c + d) % 2) for d in range(1, 8)]
    plane_dev = [device(x, z, yy, h, cc) for yy, cc in plane]
    w = 4 * h + u
    ring = [(w + d) % 8 for d in (1, 7, 2)]
    above, below, above2 = [device(x, ww % 4 * 4 + v, y, ww // 4, c) for ww in ring]
    ring_to = [above, below, above2]

    load = pltpu.make_async_copy(s_ref, abuf.at[v, x], in_sem)
    load.start()
    side_dev = [device((x + d) % 4, z, y, h, c) for d in range(1, 4)]
    line_dev = [device(x, u * 4 + (v + d) % 4, y, h, c) for d in range(1, 4)]
    barrier = pltpu.get_barrier_semaphore()
    for to in [above, below] + line_dev + side_dev + plane_dev:
        signal(barrier, to)
    load.wait()
    pl.semaphore_wait(barrier, 15)

    mine = abuf.at[v, x]

    def b_out(k):
        src = mine if isinstance(k, int) and k == 0 else bbuf.at[u2(k)]
        to = device(x, (u + way) * 4 + v, y, h, c)
        return copy(src, bbuf.at[u2(k)], b_ss.at[k], b_rs.at[u2(k)], to)

    def b_in(k):
        return copy(mine, bbuf.at[u2(k)], b_ss.at[0], b_rs.at[u2(k)], here)

    def a_out(d):
        return copy(mine, abuf.at[v, x], a_ss.at[d], a_rs.at[v], device(x, u * 4 + (v + d) % 4, y, h, c))

    def x_out(d, e):
        vv = (v + d) % 4
        src = abuf.at[vv, x]
        return copy(src, abuf.at[vv, x], x_ss.at[d, e], x_rs.at[vv, x], device((x + e) % 4, z, y, h, c))

    def relay_b(k):
        @pl.when(k < steps)
        def _():
            b_in(k).wait_recv()
            pl.when(passes)(b_out(k).start)

    def relay_a(d):
        vv = (v + d) % 4
        copy(mine, abuf.at[vv, x], a_ss.at[d], a_rs.at[vv], here).wait_recv()
        for e in (1, 3, 2):
            x_out(d, e).start()

    def take_a(d):
        vv = (v + d) % 4
        for e in range(1, 4):
            xx = (x + e) % 4
            copy(mine, abuf.at[vv, xx], x_ss.at[d, e], x_rs.at[vv, xx], here).wait_recv()
        wide = jnp.concatenate([abuf[vv, xx].astype(F32) for xx in range(4)], axis=0)
        acat[vv] = wide.astype(BF16)
        norm = jnp.sum(wide * wide, axis=1, keepdims=True)
        anorm[vv] = jnp.broadcast_to(norm, (norm.shape[0], 128))

    pl.when(passes)(b_out(0).start)
    for d in (1, 3, 2):
        a_out(d).start()
    for e in (1, 3, 2):
        x_out(0, e).start()
    signal(up_sem, above)
    signal(down_sem.at[0], below)
    for to in side_dev:
        signal(side_sem, to)
    bbuf[u] = abuf[v, x]
    relay_a(1)
    relay_b(1)
    relay_a(3)
    relay_a(2)
    pl.semaphore_wait(side_sem, 3)
    for to in near_dev:
        signal(near_sem, to)
    pl.semaphore_wait(up_sem, 1)
    pl.semaphore_wait(down_sem.at[0], 1)
    signal(down_sem.at[1], below)
    for to in plane_dev:
        signal(plane_sem, to)
    def r1_out(vv, k):
        return copy(tbuf.at[vv, k], r1buf.at[y, k], r1_ss.at[vv, k], r1_rs.at[y, k], device(x, z, vv, h, c))

    def h_out(k):
        return copy(hsend.at[k], hbuf.at[k], h_ss.at[k], h_rs.at[k], other)

    def reduce_y(k):
        for d in range(1, 4):
            yy = (y + d) % 4
            copy(tbuf.at[0, k], r1buf.at[yy, k], r1_ss.at[0, k], r1_rs.at[yy, k], here).wait_recv()
        tile = tbuf[y, k]
        for d in range(1, 4):
            tile = tile + r1buf[(y + d) % 4, k]
        hsend[k] = tile
        h_out(k).start()

    def norm_of(k):
        wide = bbuf[u2(k)].astype(F32)
        norm = jnp.sum(wide * wide, axis=1, keepdims=True)
        bnorm[k] = jnp.broadcast_to(norm, (norm.shape[0], 128)).T[0:1]

    def tile(k, d):
        vv = (v + d) % 4
        gram = lax.dot_general(acat[vv], bbuf[u2(k)], NT, preferred_element_type=F32)
        tbuf[vv, k] = pack(bnorm[k] + anorm[vv, :, :40] - 2.0 * gram)
        pl.when(vv != y)(r1_out(vv, k).start)

    def tiles(first, last, ds):
        def one(k, carry):
            for d in ds:
                tile(k, d)
            return carry

        lax.fori_loop(first, last, one, 0)

    def reduce_all(first, last):
        def one(k, carry):
            reduce_y(k)
            return carry

        lax.fori_loop(first, last, one, 0)

    three_steps = jnp.minimum(steps, 3)

    def reduce_if(d):
        pl.when((v + d) % 4 == y)(lambda: reduce_all(0, three_steps))

    pl.semaphore_wait(down_sem.at[1], 1)
    signal(down_sem.at[2], below)
    relay_b(2)
    take_a(0)
    for k in range(3):
        pl.when(k < steps)(functools.partial(norm_of, k))
    tiles(0, three_steps, (0,))
    take_a(1)
    tiles(0, three_steps, (1,))
    pl.semaphore_wait(down_sem.at[2], 1)
    reduce_if(0)
    take_a(3)
    tiles(0, three_steps, (3,))
    reduce_if(1)
    take_a(2)
    tiles(0, three_steps, (2,))
    reduce_if(3)
    pl.semaphore_wait(plane_sem, 7)
    pl.semaphore_wait(near_sem, 15)

    @pl.when(steps == 4)
    def _():
        b_in(3).wait_recv()
        norm_of(3)
        tiles(3, 4, (0, 1, 3, 2))

    reduce_if(2)
    pl.when(steps == 4)(lambda: reduce_all(3, 4))

    def sw_out(k):
        return copy(swsend.at[k], swbuf.at[y // 2], sw_ss.at[k], sw_rs.at[y // 2], swap_to(k))

    def ow_out(k, xx):
        return copy(owsend.at[k, xx], owbuf.at[v // 2, x], ow_ss.at[k, xx], ow_rs.at[v // 2, x], own_to(k, xx))

    def swaps(k):
        return jnp.logical_or(c == 0, k > 0)

    def owns(k):
        return jnp.logical_or(c == 1, k > 0)

    def place(k, carry):
        copy(hsend.at[k], hbuf.at[k], h_ss.at[k], h_rs.at[k], other).wait_recv()
        packed = hsend[k] + hbuf[k]
        swsend[k] = packed
        same = is_me(swap_to(k))

        @pl.when(both(swaps(k), same))
        def _():
            swbuf[y // 2] = swsend[k]

        pl.when(both(swaps(k), no(same)))(sw_out(k).start)

        @pl.when(owns(k))
        def _():
            turned = unpack(packed)
            for xx in range(4):
                owsend[k, xx] = pack_quarter(turned[xx * 40 : xx * 40 + 40])
                same = is_me(own_to(k, xx))

                @pl.when(same)
                def _():
                    owbuf[v // 2, x] = owsend[k, xx]

                pl.when(no(same))(ow_out(k, xx).start)

        return carry

    lax.fori_loop(0, steps, place, 0)

    for b in range(2):

        @pl.when(no(is_me(swap_from[b])))
        def _():
            copy(swsend.at[0], swbuf.at[b], sw_ss.at[0], sw_rs.at[b], here).wait_recv()

        for xx in range(4):

            @pl.when(no(is_me(own_from[b][xx])))
            def _():
                copy(owsend.at[0, 0], owbuf.at[b, xx], ow_ss.at[0, 0], ow_rs.at[b, xx], here).wait_recv()

    values = []
    for b in range(2):
        own = jnp.concatenate([unpack_quarter(owbuf[b, xx]) for xx in range(4)], axis=1)
        values.append(jnp.exp(-(unpack(swbuf[b]).T + own) / scale))

    def d1_out(i):
        return copy(d1buf.at[4 * v + x], d1buf.at[4 * v + x], d1_ss, d1_rs, near_dev[i])

    for b in range(2):
        d1buf[4 * v + x, b] = jnp.sum(values[b], axis=0, keepdims=True)
    for i in range(15):
        d1_out(i).start()
    fifteen = d1buf.at[pl.ds(0, 15)]
    copy(fifteen, fifteen, d1_ss, d1_rs, here).wait_recv()
    density = d1buf[0]
    for i in range(1, 16):
        density = density + d1buf[i]

    def d2_out(i):
        return copy(d2buf.at[u], d2buf.at[u], d2_ss, d2_rs, ring_to[i])

    d2buf[u] = density
    for i in range(3):
        d2_out(i).start()
    three = d2buf.at[pl.ds(0, 3)]
    copy(three, three, d2_ss, d2_rs, here).wait_recv()
    density = d2buf[0] + d2buf[1] + d2buf[2] + d2buf[3]

    scaled = [values[b] / density[b] for b in range(2)]
    degree = jnp.sum(scaled[0], axis=1, keepdims=True) + jnp.sum(scaled[1], axis=1, keepdims=True)
    place = 2 * y + c

    def g_out(i):
        return copy(gbuf.at[place], gbuf.at[place], g_ss, g_rs, plane_dev[i])

    gbuf[place] = jnp.broadcast_to(degree, (40, 128)).T[0:1]
    for i in range(7):
        g_out(i).start()
    for d in range(1, 4):
        a_out(d).wait_send()
    for d in range(4):
        for e in range(1, 4):
            x_out(d, e).wait_send()
    for k in range(3):
        pl.when(both(passes, k < steps))(b_out(k).wait_send)

    def sent_tiles(k, carry):
        for vv in range(4):
            pl.when(vv != y)(r1_out(vv, k).wait_send)
        h_out(k).wait_send()
        return carry

    lax.fori_loop(0, steps, sent_tiles, 0)

    def sent_places(k, carry):
        pl.when(both(swaps(k), no(is_me(swap_to(k)))))(sw_out(k).wait_send)
        for xx in range(4):
            pl.when(both(owns(k), no(is_me(own_to(k, xx)))))(ow_out(k, xx).wait_send)
        return carry

    lax.fori_loop(0, steps, sent_places, 0)

    copy(fifteen, fifteen, d1_ss, d1_rs, here).wait_send()
    copy(three, three, d2_ss, d2_rs, here).wait_send()

    seven = gbuf.at[pl.ds(0, 7)]
    copy(seven, seven, g_ss, g_rs, here).wait_recv()
    degree = gbuf[0]
    for i in range(1, 8):
        degree = degree + gbuf[i]
    degree = jnp.broadcast_to(degree, (128, 40)).T[:, 0:1]
    o_ref[...] = total * jnp.where(h == 0, scaled[0], scaled[1]) / degree

    copy(seven, seven, g_ss, g_rs, here).wait_send()


def per_device(samples):
    rows, width = samples.shape
    total = 1.0 * rows * lax.axis_size("runs")
    scale = 4.0 * width * lax.axis_size("feat")
    dma = pltpu.SemaphoreType.DMA
    regular = pltpu.SemaphoreType.REGULAR
    vm = pltpu.VMEM
    return pl.pallas_call(
        functools.partial(kernel, total, scale),
        out_shape=jax.ShapeDtypeStruct((rows, 4 * rows), F32),
        in_specs=[pl.BlockSpec(memory_space=pl.ANY)],
        out_specs=pl.BlockSpec(memory_space=pltpu.VMEM),
        scratch_shapes=[
            vm((4, 4, rows, width), BF16),
            vm((4, rows, width), BF16),
            vm((4, 4 * rows, width), BF16),
            vm((4, 4 * rows, 128), F32),
            vm((4, 1, rows), F32),
            vm((4, 4, 56, 128), F32),
            vm((4, 4, 56, 128), F32),
            vm((4, 56, 128), F32),
            vm((4, 56, 128), F32),
            vm((4, 56, 128), F32),
            vm((4, 4, 16, 128), F32),
            vm((2, 56, 128), F32),
            vm((2, 4, 16, 128), F32),
            vm((16, 2, 1, 4 * rows), F32),
            vm((4, 2, 1, 4 * rows), F32),
            vm((8, 1, rows), F32),
            dma((4,)), dma((4,)),
            dma((4, 4)), dma((4, 4)),
            dma((3,)), dma((4,)),
            dma((4, 4)), dma((4, 4)),
            dma((4,)), dma((4,)),
            dma((4,)), dma((2,)),
            dma((4, 4)), dma((2, 4)),
            dma, dma,
            dma, dma,
            dma, dma,
            regular, regular((3,)), regular, regular, regular, dma,
        ],
        compiler_params=pltpu.CompilerParams(
            collective_id=0, has_side_effects=True, vmem_limit_bytes=48 << 20
        ),
        name="markov",
    )(samples)


def solution(mesh):
    placed = P("runs", "feat")
    return jax.shard_map(per_device, mesh=mesh, in_specs=(placed,), out_specs=placed, check_vma=False)
```

time: 108 us -> 99.5 us (0.921)
  Pallas kernels: 106 us -> 97.8 us
    pallas_call x1, Pallas kernels: 106 us -> 97.8 us  [per_device(): pl.pallas_call(functools.partial(kernel, total, scale), out_shape=jax.Sha...]
where the time goes in v4:
time: 99.5 us; the launch traced here: 99.4 us
  Pallas kernels  97.8 us (98%)
  local copies, waits for them, and re-layouts  1.52 us (2%)
    pallas_call x1, Pallas kernels, per_device(): pl.pallas_call(functools.partial(kernel, total, scale), out_shape=jax.Sha...  97.8 us

profile of v4, /device:TPU:1, one launch (start us, length us, event | category | flops | bytes accessed | tf_op | source)
XLA Modules:
  0.0 99.4 jit_solution(11061094491679901757)
XLA Ops:
  0.0 0.0 copy-start
  0.0 0.9 copy-done
  0.9 97.8 %markov.1 = f32[40,160]{1,0:T(8,128)S(1)} custom-call(bf16[40,1536]{1,0:T(8,128)(2,1)S(1)} %copy-done), custom_call_target="tpu_custom_call" | custom-call | tf_op jit(solution)/shard_map/markov/pallas_call | solution.py:381
  98.8 0.6 copy.3
Async XLA Ops:
  0.0 0.9 copy-start

commit v5 on v4

--- a/solution.py
+++ b/solution.py
@@ -416,7 +416,7 @@
             collective_id=0, has_side_effects=True, vmem_limit_bytes=48 << 20
         ),
         name="markov",
-    )(samples)
+    )(pltpu.with_memory_space_constraint(samples, pltpu.HBM))
 
 
 def solution(mesh):

time: 99.5 us -> 98.4 us (0.989)
  no operation moved by 1% of the time
where the time goes in v5:
time: 98.4 us; the launch traced here: 98.3 us
  Pallas kernels  97.6 us (99%)
    pallas_call x1, Pallas kernels, per_device(): pl.pallas_call(functools.partial(kernel, total, scale), out_shape=jax.Sha...  97.6 us

profile of v5, /device:TPU:1, one launch (start us, length us, event | category | flops | bytes accessed | tf_op | source)
XLA Modules:
  0.0 98.3 jit_solution(10244784215152157368)
XLA Ops:
  0.0 97.6 %markov.1 = f32[40,160]{1,0:T(8,128)S(1)} custom-call(bf16[40,1536]{1,0:T(8,128)(2,1)} %s_ref.1), custom_call_target="tpu_custom_call" | custom-call | tf_op jit(solution)/shard_map/markov/pallas_call | solution.py:381
  97.6 0.6 copy.3
